TPU v7x, 32 devices: a whole 2x2x4 slice. The times are simulated.
32 devices in a mesh: aa: 8 (over z, x), ba: 4 (over y, core).
Axes of the slice: x: 2, y: 2, z: 4, core: 2. Of those that a mesh axis runs over, the one named last changes fastest.
Arguments:
- snapshots: float32 [2048, 8192], P(('aa', 'ba')), may hold values from -125 to 125
Outputs:
- factors: float32 [8, 16, 16], replicated
- pod_modes: float32 [8, 16, 8192], P(None, None, ('aa', 'ba'))
All inputs are finite; a program needn't handle non-finite values.
Results may differ from a plain program's by a relative error of at most 0.000098.
Values sent between devices are 32-bit elements; how exact they have to be, the bound alone decides.
A program may use at most 128 MiB of HBM per device.

v0:
```python
import math

import jax
import jax.numpy as jnp
from jax import lax
from jax.sharding import PartitionSpec as P

FREQS = 8


def spectral_table(block_len, points):
    sample = jnp.arange(block_len, dtype=jnp.int32)
    harmonic = jnp.arange(1, FREQS + 1, dtype=jnp.int32)
    phase_turns = (sample[:, None] * harmonic[None, :] % block_len).astype(jnp.float32) * (
        2.0 * math.pi / block_len
    )
    sample_angle = sample.astype(jnp.float32) * (2.0 * math.pi / block_len)
    window = 0.5 - 0.5 * jnp.cos(sample_angle)
    norm_scale = 1.0 / jnp.sqrt(points * jnp.sum(window * window))
    cosine = window[:, None] * jnp.cos(phase_turns) * norm_scale
    sine = -window[:, None] * jnp.sin(phase_turns) * norm_scale
    return jnp.stack([cosine, sine], axis=1)


def local(snapshots):
    time_dev, points = snapshots.shape
    n_aa = lax.axis_size("aa")
    n_ba = lax.axis_size("ba")
    pts_dev = points // (n_aa * n_ba)
    block_len = time_dev * n_ba
    table = spectral_table(block_len, points)
    regrouped = lax.all_to_all(
        lax.all_to_all(snapshots, "aa", split_axis=1, concat_axis=0, tiled=True),
        "ba",
        split_axis=1,
        concat_axis=0,
        tiled=True,
    )
    arranged = regrouped.reshape(n_ba, n_aa, time_dev, pts_dev)
    table_parts = table.reshape(n_ba, time_dev, 2, FREQS)
    spectra = jnp.einsum("uasp,usgf->agfp", arranged, table_parts, precision=lax.Precision.HIGHEST)
    blocks = spectra.shape[0]
    columns = 2 * blocks
    product = jnp.einsum("bgfp,chfp->fbgch", spectra, spectra, precision=lax.Precision.HIGHEST)
    gram_sum = lax.psum(product.reshape(FREQS, columns, columns), ("aa", "ba"))
    lower_factor = jnp.linalg.cholesky(gram_sum)
    identity = jnp.broadcast_to(jnp.eye(columns, dtype=gram_sum.dtype), lower_factor.shape)
    inverse = lax.linalg.triangular_solve(lower_factor, identity, left_side=True, lower=True)
    pod_modes = math.sqrt(points) * jnp.einsum(
        "fibg,bgfp->fip",
        inverse.reshape(FREQS, columns, blocks, 2),
        spectra,
        precision=lax.Precision.HIGHEST,
    )
    return (jnp.swapaxes(lower_factor, 1, 2), pod_modes)


def solution(mesh):
    placed = (P(("aa", "ba"), None),)
    return jax.shard_map(
        local,
        mesh=mesh,
        in_specs=placed,
        out_specs=(P(), P(None, None, ("aa", "ba"))),
        check_vma=False,
    )
```

profile of v0, /device:TPU:0, one launch (start us, length us, event | category | flops | bytes accessed | tf_op | source)
XLA Modules:
  0.0 157.8 jit_solution(16909486269220759021)
XLA Ops:
  0.6 1.7 %copy.74 = f32[8,8,8,1024]{3,2,0,1:T(8,128)S(1)} copy(f32[8,8,8,1024]{3,2,1,0:T(8,128)} %bitcast.46) | data formatting | bytes 4194304 | tf_op jit(solution)/shard_map/all_to_all | solution.py:33
  2.4 55.3 %all_to_all.32 = f32[64,8,1024]{2,0,1:T(8,128)S(1)} all-to-all(f32[64,8,1024]{2,0,1:T(8,128)S(1)} %bitcast.43), channel_id=1, replica_groups=mesh['aa'=8,'ba'=4] {'aa'}, dimensions={1} | all-to-all | bytes 4194304 | tf_op jit(solution)/shard_map/all_to_all | solution.py:33
  57.7 2.0 %all_to_all.27 = f32[512,4,256]{2,1,0:T(4,128)} reshape(f32[8,64,1024]{2,1,0:T(8,128)S(1)} %bitcast.42) | data formatting | bytes 4194304 | tf_op jit(solution)/shard_map/all_to_all | solution.py:32
  59.7 3.3 %copy.38 = f32[512,4,256]{2,0,1:T(8,128)} copy(f32[512,4,256]{2,1,0:T(4,128)} %all_to_all.27) | data formatting | bytes 4194304 | tf_op jit(solution)/shard_map/all_to_all | solution.py:32
  63.0 3.6 %all-to-all-start.1 = ((f32[512,4,256]{2,0,1:T(8,128)}), f32[512,4,256]{2,0,1:T(8,128)S(1)}, u32[]{:S(2)}, u32[]{:S(2)}) async-start(f32[512,4,256]{2,0,1:T(8,128)} %copy.38), calls=%async_computation.1 | async-start | bytes 4194304 | tf_op jit(solution)/shard_map/all_to_all | solution.py:32
  66.6 0.6 multiply_reduce_fusion
  68.0 0.2 multiply_multiply_fusion.1
  68.2 24.1 %all-to-all-done.1 = f32[512,4,256]{2,0,1:T(8,128)S(1)} async-done(((f32[512,4,256]{2,0,1:T(8,128)}), f32[512,4,256]{2,0,1:T(8,128)S(1)}, u32[]{:S(2)}, u32[]{:S(2)}) %all-to-all-start.1) | async-done | bytes 2097184 | tf_op jit(solution)/shard_map/all_to_all | solution.py:32
  92.3 1.1 fusion
  93.4 1.0 fusion.4
  94.3 0.2 copy.42
  94.5 0.1 copy.43
  94.6 39.1 %psum.7 = f32[8,16,16]{1,2,0:T(8,128)S(1)} all-reduce(f32[8,16,16]{1,2,0:T(8,128)S(1)} %copy.43), channel_id=1, replica_groups=mesh['aa'=8,'ba'=4] {'aa','ba'}, use_global_device_ids=true, to_apply=%region_1.2 | all-reduce | flops 2048 | bytes 16384 | tf_op jit(solution)/shard_map/psum | solution.py:45
  133.8 0.1 copy.44
  133.9 11.7 %custom-call.7 = f32[8,16,16]{2,1,0:T(8,128)S(1)} custom-call(f32[8,16,16]{2,1,0:T(8,128)S(1)} %fusion.10), custom_call_target="Cholesky" | custom-call | tf_op jit(solution)/shard_map/jit(cholesky)/cholesky | solution.py:46
  145.6 0.1 compare_reduce_fusion
  145.8 0.1 select_bitcast_fusion
  145.8 0.7 copy.49
  146.6 9.8 %custom-call.8 = f32[8,1,16,16]{2,3,1,0:T(8,128)S(1)} custom-call(f32[8,1,16,16]{3,2,1,0:T(8,128)S(1)} %get-tuple-element.10), custom_call_target="InvertDiagBlocksLowerTriangular" | custom-call | tf_op jit(solution)/shard_map/triangular_solve | solution.py:48
  156.4 0.4 fusion.8
  156.8 0.1 copy.46
  156.9 1.0 fusion.3
  (8 shorter events, 0.1 us)
Async XLA Ops:
  63.0 29.3 %all-to-all-start.1 = ((f32[512,4,256]{2,0,1:T(8,128)}), f32[512,4,256]{2,0,1:T(8,128)S(1)}, u32[]{:S(2)}, u32[]{:S(2)}) async-start(f32[512,4,256]{2,0,1:T(8,128)} %copy.38), calls=%async_computation.1 | async-start | bytes 4194304 | tf_op jit(solution)/shard_map/all_to_all | solution.py:32
where the time goes:
time: 158 us
  blocking collectives  94.4 us (60%)
  waiting for transfers between devices  24.1 us (15%)
  other arithmetic  22.7 us (14%)
  local copies, waits for them, and re-layouts  8.2 us (5%)
  starting transfers between devices  3.61 us (2%)
  matrix products  3.44 us (2%)
    all_to_all x1, blocking collectives, local(): lax.all_to_all(snapshots, 'aa', split_axis=1, concat_axis=0, tiled=True)  55.3 us
    psum x1, blocking collectives, local(): gram_sum = lax.psum(product.reshape(FREQS, columns, columns), ('aa', 'ba'))  39.1 us
    all_to_all x1, waiting for transfers between devices, local(): lax.all_to_all(lax.all_to_all(snapshots, 'aa', split_axis=1, concat_axis=...  24.1 us
    another operation x4, other arithmetic, local(): lower_factor = jnp.linalg.cholesky(gram_sum)  11.9 us
    another operation x2, other arithmetic, local(): lax.linalg.triangular_solve(lower_factor, identity, left_side=True, lower...  9.91 us
    all_to_all x2, local copies, waits for them, and re-layouts, local(): lax.all_to_all(lax.all_to_all(snapshots, 'aa', split_axis=1, concat_axis=...  5.32 us
    all_to_all x1, starting transfers between devices, local(): lax.all_to_all(lax.all_to_all(snapshots, 'aa', split_axis=1, concat_axis=...  3.61 us
  transfers between devices with their start and end apart: 1, of which 1 were waited for; matrix products, arithmetic and copies ran while one was open for 1% of the time, Pallas kernels for 0%

commit v1 on v0

--- a/solution.py
+++ b/solution.py
@@ -1,11 +1,22 @@
+import functools
 import math
 
 import jax
 import jax.numpy as jnp
+import ml_dtypes
+import numpy as np
 from jax import lax
+from jax.experimental import pallas as pl
+from jax.experimental.pallas import tpu as pltpu
 from jax.sharding import PartitionSpec as P
 
 FREQS = 8
+MESH = pl.DeviceIdType.MESH
+BF16 = jnp.bfloat16
+F32 = jnp.float32
+
+STEPS = ((2, 0), (2, 1), (1, 0), (1, 1), (3, 0), (3, 1), (0, 1), (0, 0))
+LAG = 6
 
 
 def spectral_table(block_len, points):
@@ -22,10 +33,259 @@
     return jnp.stack([cosine, sine], axis=1)
 
 
+def split_table(block_len, points, parts):
+    sample = np.arange(block_len)
+    harmonic = np.arange(1, FREQS + 1)
+    turns = (harmonic[:, None] * sample[None, :] % block_len) * (2.0 * np.pi / block_len)
+    window = 0.5 - 0.5 * np.cos(sample * (2.0 * np.pi / block_len))
+    scale = window / np.sqrt(points * np.sum(window * window))
+    full = np.stack([np.cos(turns) * scale, -np.sin(turns) * scale], axis=1)
+    full = full.reshape(2 * FREQS, parts, block_len // parts).transpose(1, 0, 2).astype(np.float32)
+    terms = []
+    rest = full
+    for _ in range(3):
+        term = rest.astype(ml_dtypes.bfloat16)
+        terms.append(term)
+        rest = rest - term.astype(np.float32)
+    rows = np.concatenate(terms, axis=1)
+    return np.concatenate([rows] * 3, axis=2)
+
+
+def split3(value):
+    high = value.astype(BF16)
+    rest = value - high.astype(F32)
+    middle = rest.astype(BF16)
+    low = (rest - middle.astype(F32)).astype(BF16)
+    return high, middle, low
+
+
+def kernel(
+    points, x_hbm, table_hbm, factors_ref, modes_ref,
+    x_buf, table, part, core_in, y_out, y_in, block_out, blocks,
+    gram_out, gram_in, plane_out, plane_in, upper,
+    in_sem, table_sem, core_send, core_recv, y_send, y_recv,
+    block_send, block_recv, gram_send, gram_recv, plane_send, plane_recv,
+):
+    aa, ba = lax.axis_index("aa"), lax.axis_index("ba")
+    z, x = aa // 2, aa % 2
+    y, core = ba // 2, ba % 2
+    other_core = 1 - core
+    core_peer = (aa, y * 2 + other_core)
+    y_peer = (aa, (1 - y) * 2 + core)
+    owners = [((z + dz) % 4) * 2 + (x + dx) % 2 for dz, dx in STEPS]
+    plane = [(i // 4, i // 2 % 2, i % 2) for i in range(8)]
+    plane_ids = [
+        (z * 2 + (x + dx) % 2, ((y + dy) % 2) * 2 + (core + dc) % 2) for dx, dy, dc in plane
+    ]
+    line_ids = [(((z + dz) % 4) * 2 + x, ba) for dz in range(4)]
+
+    barrier = pltpu.get_barrier_semaphore()
+    peers = [(owner, ba) for owner in owners[:-1]]
+    peers += [plane_ids[i] for i in range(1, 8) if plane[i] != (1, 0, 0)]
+    for peer in peers:
+        pl.semaphore_signal(barrier, inc=1, device_id=peer, device_id_type=MESH)
+
+    table_copy = pltpu.make_async_copy(table_hbm.at[ba], table, table_sem)
+    table_copy.start()
+    loads = []
+    for tile in range(16):
+        row, k = tile // 8, tile % 8
+        side = (1 - y) if row == 0 else y
+        start = pl.multiple_of(owners[k] * 1024 + side * 512, 512)
+        load = pltpu.make_async_copy(x_hbm.at[:, pl.ds(start, 512)], x_buf.at[tile], in_sem.at[tile])
+        load.start()
+        loads.append(load)
+    table_copy.wait()
+
+    sends = []
+
+    def remote(src, dst, send, recv, device):
+        copy = pltpu.make_async_remote_copy(
+            src_ref=src, dst_ref=dst, send_sem=send, recv_sem=recv,
+            device_id=device, device_id_type=MESH,
+        )
+        copy.start()
+        sends.append(copy)
+        return copy
+
+    core_copies = []
+    y_copies = []
+
+    def send_y(k):
+        core_copies[k].wait_recv()
+        y_out[k] = part[k, core] + core_in[k]
+        y_copies.append(remote(y_out.at[k], y_in.at[k], y_send.at[k], y_recv.at[k], y_peer))
+
+    for tile in range(16):
+        loads[tile].wait()
+        terms = jnp.concatenate(split3(x_buf[tile]), axis=0)
+        rows = jnp.dot(table[...], terms, preferred_element_type=F32)
+        total = rows[0:16] + rows[16:32] + rows[32:48]
+        part[tile, 0] = total[:, 0:256]
+        part[tile, 1] = total[:, 256:512]
+        if tile == 0:
+            pl.semaphore_wait(barrier, len(peers))
+        core_copies.append(
+            remote(
+                part.at[tile, other_core], core_in.at[tile],
+                core_send.at[tile], core_recv.at[tile], core_peer,
+            )
+        )
+        if LAG <= tile < LAG + 8:
+            send_y(tile - LAG)
+
+    block_copies = []
+    for k in range(8):
+        core_copies[8 + k].wait_recv()
+        y_copies[k].wait_recv()
+        total = part[8 + k, core] + core_in[8 + k] + y_in[k]
+        mine = pl.ds(pl.multiple_of(aa * 16, 16), 16)
+        if k == 7:
+            blocks[0, mine, :] = total[:, 0:128]
+            blocks[1, mine, :] = total[:, 128:256]
+        else:
+            block_out[k, 0] = total[:, 0:128]
+            block_out[k, 1] = total[:, 128:256]
+            block_copies.append(
+                remote(
+                    block_out.at[k], blocks.at[:, mine, :],
+                    block_send.at[k], block_recv.at[k], (owners[k], ba),
+                )
+            )
+    for copy in block_copies:
+        copy.wait_recv()
+
+    columns = jnp.concatenate(
+        [
+            jnp.concatenate([blocks[half, pl.ds(r, 8, stride=16), :] for r in range(16)], axis=0)
+            for half in range(2)
+        ],
+        axis=1,
+    )
+    high, middle, low = split3(columns)
+    gram_full = lax.dot_general(
+        jnp.concatenate([high, high, middle, middle, high, low], axis=1),
+        jnp.concatenate([high, middle, high, middle, low, high], axis=1),
+        (((1,), (1,)), ((), ())),
+        preferred_element_type=F32,
+    )
+    row_freq = lax.broadcasted_iota(jnp.int32, (128, 128), 0) // 16
+    lane_freq = lax.broadcasted_iota(jnp.int32, (128, 128), 1) // 16
+    same = row_freq == lane_freq
+    kept = jnp.where(same, gram_full, 0.0).reshape(8, 16, 128)
+    gram_out[...] = ((kept[0] + kept[1]) + (kept[2] + kept[3])) + ((kept[4] + kept[5]) + (kept[6] + kept[7]))
+
+    copies = [
+        remote(gram_out, gram_in.at[i], gram_send.at[i], gram_recv.at[i], plane_ids[i]) for i in range(1, 8)
+    ]
+    for copy in copies:
+        copy.wait_recv()
+    pairs = [gram_out[...] + gram_in[1]] + [gram_in[i] + gram_in[i + 1] for i in (2, 4, 6)]
+    plane_out[...] = (pairs[0] + pairs[1]) + (pairs[2] + pairs[3])
+    copies = [
+        remote(plane_out, plane_in.at[i], plane_send.at[i], plane_recv.at[i], line_ids[i]) for i in range(1, 4)
+    ]
+    for copy in copies:
+        copy.wait_recv()
+    gram = (plane_out[...] + plane_in[2]) + (plane_in[1] + plane_in[3])
+
+    lane = lax.broadcasted_iota(jnp.int32, (16, 128), 1) % 16
+    row = lax.broadcasted_iota(jnp.int32, (16, 128), 0)
+    natural = (row % 8) * 2 + row // 8
+    place = [(j % 2) * 8 + j // 2 for j in range(16)]
+    left = [pltpu.roll(gram, (128 - place[j]) % 128, 1) if place[j] else gram for j in range(16)]
+    right = [(row == place[j]).astype(F32) for j in range(16)]
+    upper_all = jnp.zeros((16, 128), F32)
+    inverse_all = jnp.zeros((16, 128), F32)
+    for j in range(16):
+        pivot = left[j][place[j]:place[j] + 1, :]
+        root = lax.rsqrt(pivot)
+        root = root * (1.5 - 0.5 * pivot * root * root)
+        upper_row = left[j] * root
+        inverse_row = right[j] * root
+        for i in range(j + 1, 16):
+            scale = upper_row[place[i]:place[i] + 1, :]
+            left[i] = left[i] - scale * upper_row
+            right[i] = right[i] - scale * inverse_row
+        upper_row = jnp.where(natural >= j, upper_row, 0.0)
+        if j:
+            upper_row = pltpu.roll(upper_row, j, 1)
+            inverse_row = pltpu.roll(inverse_row, j, 1)
+        upper_all = jnp.where(lane == j, upper_row, upper_all)
+        inverse_all = jnp.where(lane == j, inverse_row, inverse_all)
+
+    upper[...] = jnp.zeros_like(upper)
+    upper[pl.ds(0, 8, stride=2), :] = upper_all[0:8]
+    upper[pl.ds(1, 8, stride=2), :] = upper_all[8:16]
+    factors_ref[...] = jnp.transpose(upper[...])[:, 0:16].reshape(8, 16, 16)
+
+    inverse_all = inverse_all * math.sqrt(points)
+    wide = jnp.where(same, jnp.concatenate([inverse_all] * 8, axis=0), 0.0)
+    w_high, w_middle, w_low = split3(jnp.transpose(wide))
+    modes = lax.dot_general(
+        jnp.concatenate([w_high, w_high, w_middle, w_middle, w_high, w_low], axis=1),
+        jnp.concatenate([high, middle, high, middle, low, high], axis=0),
+        (((1,), (0,)), ((), ())),
+        preferred_element_type=F32,
+    )
+    modes_ref[...] = modes.reshape(8, 16, 256)
+    for copy in sends:
+        copy.wait_send()
+
+
+def fused(snapshots):
+    points = snapshots.shape[1]
+    table = jnp.asarray(split_table(256, points, 4))
+    dma = pltpu.SemaphoreType.DMA
+    vmem = pltpu.VMEM
+    return pl.pallas_call(
+        functools.partial(kernel, points),
+        out_shape=(
+            jax.ShapeDtypeStruct((8, 16, 16), F32),
+            jax.ShapeDtypeStruct((8, 16, 256), F32),
+        ),
+        in_specs=[pl.BlockSpec(memory_space=pl.ANY)] * 2,
+        out_specs=(pl.BlockSpec(memory_space=pltpu.VMEM),) * 2,
+        scratch_shapes=[
+            vmem((16, 64, 512), F32),
+            vmem((48, 192), BF16),
+            vmem((16, 2, 16, 256), F32),
+            vmem((16, 16, 256), F32),
+            vmem((8, 16, 256), F32),
+            vmem((8, 16, 256), F32),
+            vmem((8, 2, 16, 128), F32),
+            vmem((2, 128, 128), F32),
+            vmem((16, 128), F32),
+            vmem((8, 16, 128), F32),
+            vmem((16, 128), F32),
+            vmem((4, 16, 128), F32),
+            vmem((128, 128), F32),
+            dma((16,)),
+            dma,
+            dma((16,)),
+            dma((16,)),
+            dma((8,)),
+            dma((8,)),
+            dma((8,)),
+            dma((8,)),
+            dma((8,)),
+            dma((8,)),
+            dma((4,)),
+            dma((4,)),
+        ],
+        compiler_params=pltpu.CompilerParams(
+            collective_id=0, has_side_effects=True, vmem_limit_bytes=48 * 1024 * 1024
+        ),
+        name="welch_qr",
+    )(snapshots, table)
+
+
 def local(snapshots):
     time_dev, points = snapshots.shape
     n_aa = lax.axis_size("aa")
     n_ba = lax.axis_size("ba")
+    if (n_aa, n_ba, time_dev, points) == (8, 4, 64, 8192):
+        return fused(snapshots)
     pts_dev = points // (n_aa * n_ba)
     block_len = time_dev * n_ba
     table = spectral_table(block_len, points)

time: 158 us -> 29 us (0.18)
  blocking collectives: 94.4 us -> 0 us
  Pallas kernels: 0 us -> 24.4 us
  waiting for transfers between devices: 24.1 us -> 0 us
  other arithmetic: 22.7 us -> 0 us
  local copies, waits for them, and re-layouts: 8.2 us -> 3.76 us
  starting transfers between devices: 3.61 us -> 0 us
  matrix products: 3.44 us -> 0 us
    all_to_all x1 -> x0, blocking collectives: 55.3 us -> none  [local(): lax.all_to_all(snapshots, 'aa', split_axis=1, concat_axis=0, tiled=True)]
    psum x1 -> x0, blocking collectives: 39.1 us -> none  [local(): gram_sum = lax.psum(product.reshape(FREQS, columns, columns), ('aa', 'ba'))]
    pallas_call x0 -> x1, Pallas kernels: none -> 24.4 us  [fused(): pl.pallas_call(functools.partial(kernel, points), out_shape=(jax.ShapeDty...]
    all_to_all x1 -> x0, waiting for transfers between devices: 24.1 us -> none  [local(): lax.all_to_all(lax.all_to_all(snapshots, 'aa', split_axis=1, concat_axis=...]
    another operation x6 -> x0, other arithmetic: 21.8 us -> none  [the longest x4 11.9 us: local(): lower_factor = jnp.linalg.cholesky(gram_sum)]
    all_to_all x3 -> x0, local copies, waits for them, and re-layouts: 7.05 us -> none  [the longest x2 5.32 us: local(): lax.all_to_all(lax.all_to_all(snapshots, 'aa', split_axis=1, concat_axis=...]
    all_to_all x1 -> x0, starting transfers between devices: 3.61 us -> none  [local(): lax.all_to_all(lax.all_to_all(snapshots, 'aa', split_axis=1, concat_axis=...]
    dot_general x3 -> x0, matrix products: 3.06 us -> none  [the longest x1 1.1 us: local(): jnp.einsum('uasp,usgf->agfp', arranged, table_parts, precision=lax.Precis...]
  transfers between devices with their start and end apart: 1 -> 0, of which waited for: 1 -> 0; matrix products, arithmetic and copies ran while one was open for 1% -> 0% of each run, Pallas kernels for 0% -> 0%
where the time goes in v1:
time: 29 us; the launch traced here: 28.8 us
  Pallas kernels  24.4 us (84%)
  local copies, waits for them, and re-layouts  3.76 us (13%)
  between operations  0.65 us (2%)
    pallas_call x1, Pallas kernels, fused(): pl.pallas_call(functools.partial(kernel, points), out_shape=(jax.ShapeDty...  24.4 us
    unnamed x6, local copies, waits for them, and re-layouts  3.76 us

profile of v1, /device:TPU:0, one launch (start us, length us, event | category | flops | bytes accessed | tf_op | source)
XLA Modules:
  0.0 28.8 jit_solution(10602448048092932071)
XLA Ops:
  0.6 0.0 copy-start
  0.6 1.6 %copy-done = f32[64,8192]{1,0:T(8,128)S(1)} copy-done((f32[64,8192]{1,0:T(8,128)S(1)}, f32[64,8192]{1,0:T(8,128)}, u32[]{:S(2)}) %copy-start) | copy-done | bytes 2097176
  2.2 0.0 copy-start.1
  2.2 0.9 %copy-done.1 = bf16[4,48,192]{2,1,0:T(8,128)(2,1)S(1)} copy-done((bf16[4,48,192]{2,1,0:T(8,128)(2,1)S(1)}, bf16[4,48,192]{2,1,0:T(8,128)(2,1)}, u32[]{:S(2)}) %copy-start.1) | copy-done | bytes 73752
  3.1 24.4 %welch_qr.1 = (f32[8,16,16]{2,1,0:T(8,128)S(1)}, f32[8,16,256]{2,1,0:T(8,128)S(1)}) custom-call(f32[64,8192]{1,0:T(8,128)S(1)} %copy-done, bf16[4,48,192]{2,1,0:T(8,128)(2,1)S(1)} %copy-done.1), custom_call_target="tpu_custom_call" | custom-call | tf_op jit(solution)/shard_map/welch_qr/pallas_call | solution.py:241
  27.5 0.6 %copy.6 = f32[8,16,16]{2,1,0:T(8,128)} copy(f32[8,16,16]{2,1,0:T(8,128)S(1)} %get-tuple-element.4) | data formatting | bytes 16384
  28.1 0.7 %copy.7 = f32[8,16,256]{2,1,0:T(8,128)} copy(f32[8,16,256]{2,1,0:T(8,128)S(1)} %get-tuple-element.5) | data formatting | bytes 262144
Async XLA Ops:
  0.6 1.6 %copy-start = (f32[64,8192]{1,0:T(8,128)S(1)}, f32[64,8192]{1,0:T(8,128)}, u32[]{:S(2)}) copy-start(f32[64,8192]{1,0:T(8,128)} %x_hbm.1) | copy-start | bytes 6291460
  2.2 0.9 %copy-start.1 = (bf16[4,48,192]{2,1,0:T(8,128)(2,1)S(1)}, bf16[4,48,192]{2,1,0:T(8,128)(2,1)}, u32[]{:S(2)}) copy-start(bf16[4,48,192]{2,1,0:T(8,128)(2,1)} %constant.2.clone.table_hbm) | copy-start | bytes 221188

commit v2 on v1

--- a/solution.py
+++ b/solution.py
@@ -16,7 +16,13 @@
 F32 = jnp.float32
 
 STEPS = ((2, 0), (2, 1), (1, 0), (1, 1), (3, 0), (3, 1), (0, 1), (0, 0))
-LAG = 6
+GROUPS = (
+    ((0, 1), ()),
+    ((2, 3), ()),
+    ((4, 5, 6, 7), (0, 1, 2, 3)),
+    ((8, 9, 10, 11), (4, 5, 6, 7)),
+    ((12, 13, 14, 15), ()),
+)
 
 
 def spectral_table(block_len, points):
@@ -79,12 +85,6 @@
     ]
     line_ids = [(((z + dz) % 4) * 2 + x, ba) for dz in range(4)]
 
-    barrier = pltpu.get_barrier_semaphore()
-    peers = [(owner, ba) for owner in owners[:-1]]
-    peers += [plane_ids[i] for i in range(1, 8) if plane[i] != (1, 0, 0)]
-    for peer in peers:
-        pl.semaphore_signal(barrier, inc=1, device_id=peer, device_id_type=MESH)
-
     table_copy = pltpu.make_async_copy(table_hbm.at[ba], table, table_sem)
     table_copy.start()
     loads = []
@@ -95,6 +95,12 @@
         load = pltpu.make_async_copy(x_hbm.at[:, pl.ds(start, 512)], x_buf.at[tile], in_sem.at[tile])
         load.start()
         loads.append(load)
+
+    barrier = pltpu.get_barrier_semaphore()
+    peers = [(owner, ba) for owner in owners[:-1]]
+    peers += [plane_ids[i] for i in range(1, 8) if plane[i] != (1, 0, 0)]
+    for peer in peers:
+        pl.semaphore_signal(barrier, inc=1, device_id=peer, device_id_type=MESH)
     table_copy.wait()
 
     sends = []
@@ -116,23 +122,26 @@
         y_out[k] = part[k, core] + core_in[k]
         y_copies.append(remote(y_out.at[k], y_in.at[k], y_send.at[k], y_recv.at[k], y_peer))
 
-    for tile in range(16):
-        loads[tile].wait()
-        terms = jnp.concatenate(split3(x_buf[tile]), axis=0)
-        rows = jnp.dot(table[...], terms, preferred_element_type=F32)
+    for group, ready in GROUPS:
+        for tile in group:
+            loads[tile].wait()
+        terms = [jnp.concatenate(split3(x_buf[tile]), axis=0) for tile in group]
+        rows = jnp.dot(table[...], jnp.concatenate(terms, axis=1), preferred_element_type=F32)
         total = rows[0:16] + rows[16:32] + rows[32:48]
-        part[tile, 0] = total[:, 0:256]
-        part[tile, 1] = total[:, 256:512]
-        if tile == 0:
+        for n, tile in enumerate(group):
+            part[tile, 0] = total[:, n * 512:n * 512 + 256]
+            part[tile, 1] = total[:, n * 512 + 256:n * 512 + 512]
+        if group[0] == 0:
             pl.semaphore_wait(barrier, len(peers))
-        core_copies.append(
-            remote(
-                part.at[tile, other_core], core_in.at[tile],
-                core_send.at[tile], core_recv.at[tile], core_peer,
+        for tile in group:
+            core_copies.append(
+                remote(
+                    part.at[tile, other_core], core_in.at[tile],
+                    core_send.at[tile], core_recv.at[tile], core_peer,
+                )
             )
-        )
-        if LAG <= tile < LAG + 8:
-            send_y(tile - LAG)
+        for k in ready:
+            send_y(k)
 
     block_copies = []
     for k in range(8):
@@ -163,11 +172,16 @@
         axis=1,
     )
     high, middle, low = split3(columns)
-    gram_full = lax.dot_general(
-        jnp.concatenate([high, high, middle, middle, high, low], axis=1),
-        jnp.concatenate([high, middle, high, middle, low, high], axis=1),
-        (((1,), (1,)), ((), ())),
+    contract_last = (((1,), (1,)), ((), ()))
+    product = lax.dot_general(
+        jnp.concatenate([high, middle, low], axis=0),
+        jnp.concatenate([high, middle], axis=0),
+        contract_last,
         preferred_element_type=F32,
+    )
+    high_low = lax.dot_general(high, low, contract_last, preferred_element_type=F32)
+    gram_full = (product[0:128, 0:128] + product[128:256, 128:256]) + (
+        (product[0:128, 128:256] + product[128:256, 0:128]) + (product[256:384, 0:128] + high_low)
     )
     row_freq = lax.broadcasted_iota(jnp.int32, (128, 128), 0) // 16
     lane_freq = lax.broadcasted_iota(jnp.int32, (128, 128), 1) // 16
@@ -244,7 +258,7 @@
             jax.ShapeDtypeStruct((8, 16, 16), F32),
             jax.ShapeDtypeStruct((8, 16, 256), F32),
         ),
-        in_specs=[pl.BlockSpec(memory_space=pl.ANY)] * 2,
+        in_specs=[pl.BlockSpec(memory_space=pltpu.HBM)] * 2,
         out_specs=(pl.BlockSpec(memory_space=pltpu.VMEM),) * 2,
         scratch_shapes=[
             vmem((16, 64, 512), F32),

time: 29 us -> 29 us (level)
  no operation moved by 1% of the time
where the time goes in v2:
time: 29 us; the launch traced here: 28.8 us
  Pallas kernels  24.4 us (84%)
  local copies, waits for them, and re-layouts  3.76 us (13%)
  between operations  0.65 us (2%)
    pallas_call x1, Pallas kernels, fused(): pl.pallas_call(functools.partial(kernel, points), out_shape=(jax.ShapeDty...  24.4 us
    unnamed x6, local copies, waits for them, and re-layouts  3.76 us

profile of v2, /device:TPU:0, one launch (start us, length us, event | category | flops | bytes accessed | tf_op | source)
XLA Modules:
  0.0 28.8 jit_solution(8147455933221259592)
XLA Ops:
  0.6 0.0 copy-start
  0.6 1.6 %copy-done = f32[64,8192]{1,0:T(8,128)S(1)} copy-done((f32[64,8192]{1,0:T(8,128)S(1)}, f32[64,8192]{1,0:T(8,128)}, u32[]{:S(2)}) %copy-start) | copy-done | bytes 2097176
  2.2 0.0 copy-start.1
  2.2 0.9 %copy-done.1 = bf16[4,48,192]{2,1,0:T(8,128)(2,1)S(1)} copy-done((bf16[4,48,192]{2,1,0:T(8,128)(2,1)S(1)}, bf16[4,48,192]{2,1,0:T(8,128)(2,1)}, u32[]{:S(2)}) %copy-start.1) | copy-done | bytes 73752
  3.1 24.4 %welch_qr.1 = (f32[8,16,16]{2,1,0:T(8,128)S(1)}, f32[8,16,256]{2,1,0:T(8,128)S(1)}) custom-call(f32[64,8192]{1,0:T(8,128)S(1)} %copy-done, bf16[4,48,192]{2,1,0:T(8,128)(2,1)S(1)} %copy-done.1), custom_call_target="tpu_custom_call" | custom-call | tf_op jit(solution)/shard_map/welch_qr/pallas_call | solution.py:255
  27.5 0.6 %copy.6 = f32[8,16,16]{2,1,0:T(8,128)} copy(f32[8,16,16]{2,1,0:T(8,128)S(1)} %get-tuple-element.4) | data formatting | bytes 16384
  28.1 0.7 %copy.7 = f32[8,16,256]{2,1,0:T(8,128)} copy(f32[8,16,256]{2,1,0:T(8,128)S(1)} %get-tuple-element.5) | data formatting | bytes 262144
Async XLA Ops:
  0.6 1.6 %copy-start = (f32[64,8192]{1,0:T(8,128)S(1)}, f32[64,8192]{1,0:T(8,128)}, u32[]{:S(2)}) copy-start(f32[64,8192]{1,0:T(8,128)} %x_hbm.1) | copy-start | bytes 6291460
  2.2 0.9 %copy-start.1 = (bf16[4,48,192]{2,1,0:T(8,128)(2,1)S(1)}, bf16[4,48,192]{2,1,0:T(8,128)(2,1)}, u32[]{:S(2)}) copy-start(bf16[4,48,192]{2,1,0:T(8,128)(2,1)} %constant.2.clone.table_hbm) | copy-start | bytes 221188

commit v3 on v2

--- a/solution.py
+++ b/solution.py
@@ -3,8 +3,6 @@
 
 import jax
 import jax.numpy as jnp
-import ml_dtypes
-import numpy as np
 from jax import lax
 from jax.experimental import pallas as pl
 from jax.experimental.pallas import tpu as pltpu
@@ -39,22 +37,16 @@
     return jnp.stack([cosine, sine], axis=1)
 
 
-def split_table(block_len, points, parts):
-    sample = np.arange(block_len)
-    harmonic = np.arange(1, FREQS + 1)
-    turns = (harmonic[:, None] * sample[None, :] % block_len) * (2.0 * np.pi / block_len)
-    window = 0.5 - 0.5 * np.cos(sample * (2.0 * np.pi / block_len))
-    scale = window / np.sqrt(points * np.sum(window * window))
-    full = np.stack([np.cos(turns) * scale, -np.sin(turns) * scale], axis=1)
-    full = full.reshape(2 * FREQS, parts, block_len // parts).transpose(1, 0, 2).astype(np.float32)
-    terms = []
-    rest = full
-    for _ in range(3):
-        term = rest.astype(ml_dtypes.bfloat16)
-        terms.append(term)
-        rest = rest - term.astype(np.float32)
-    rows = np.concatenate(terms, axis=1)
-    return np.concatenate([rows] * 3, axis=2)
+def split_table(ba, points):
+    row = lax.broadcasted_iota(jnp.int32, (16, 64), 0)
+    sample = lax.broadcasted_iota(jnp.int32, (16, 64), 1) + ba * 64
+    turns = (sample * (row // 2 + 1) + 64 * (row % 2)) % 256
+    step = 2.0 * math.pi / 256
+    window = 0.5 - 0.5 * jnp.cos(sample.astype(F32) * step)
+    power = sum((0.5 - 0.5 * math.cos(n * step)) ** 2 for n in range(256))
+    value = window * jnp.cos(turns.astype(F32) * step) * (1.0 / math.sqrt(points * power))
+    rows = jnp.concatenate(split3(value), axis=0)
+    return jnp.concatenate([rows] * 3, axis=1)
 
 
 def split3(value):
@@ -66,10 +58,10 @@
 
 
 def kernel(
-    points, x_hbm, table_hbm, factors_ref, modes_ref,
+    points, x_hbm, factors_ref, modes_ref,
     x_buf, table, part, core_in, y_out, y_in, block_out, blocks,
     gram_out, gram_in, plane_out, plane_in, upper,
-    in_sem, table_sem, core_send, core_recv, y_send, y_recv,
+    in_sem, core_send, core_recv, y_send, y_recv,
     block_send, block_recv, gram_send, gram_recv, plane_send, plane_recv,
 ):
     aa, ba = lax.axis_index("aa"), lax.axis_index("ba")
@@ -85,8 +77,6 @@
     ]
     line_ids = [(((z + dz) % 4) * 2 + x, ba) for dz in range(4)]
 
-    table_copy = pltpu.make_async_copy(table_hbm.at[ba], table, table_sem)
-    table_copy.start()
     loads = []
     for tile in range(16):
         row, k = tile // 8, tile % 8
@@ -101,7 +91,7 @@
     peers += [plane_ids[i] for i in range(1, 8) if plane[i] != (1, 0, 0)]
     for peer in peers:
         pl.semaphore_signal(barrier, inc=1, device_id=peer, device_id_type=MESH)
-    table_copy.wait()
+    table[...] = split_table(ba, points)
 
     sends = []
 
@@ -249,7 +239,6 @@
 
 def fused(snapshots):
     points = snapshots.shape[1]
-    table = jnp.asarray(split_table(256, points, 4))
     dma = pltpu.SemaphoreType.DMA
     vmem = pltpu.VMEM
     return pl.pallas_call(
@@ -258,7 +247,7 @@
             jax.ShapeDtypeStruct((8, 16, 16), F32),
             jax.ShapeDtypeStruct((8, 16, 256), F32),
         ),
-        in_specs=[pl.BlockSpec(memory_space=pltpu.HBM)] * 2,
+        in_specs=[pl.BlockSpec(memory_space=pltpu.HBM)],
         out_specs=(pl.BlockSpec(memory_space=pltpu.VMEM),) * 2,
         scratch_shapes=[
             vmem((16, 64, 512), F32),
@@ -275,7 +264,6 @@
             vmem((4, 16, 128), F32),
             vmem((128, 128), F32),
             dma((16,)),
-            dma,
             dma((16,)),
             dma((16,)),
             dma((8,)),
@@ -288,10 +276,10 @@
             dma((4,)),
         ],
         compiler_params=pltpu.CompilerParams(
-            collective_id=0, has_side_effects=True, vmem_limit_bytes=48 * 1024 * 1024
+            collective_id=0, has_side_effects=True, vmem_limit_bytes=63 * 1024 * 1024
         ),
         name="welch_qr",
-    )(snapshots, table)
+    )(snapshots)
 
 
 def local(snapshots):

time: 29 us -> 28.6 us (0.986)
  local copies, waits for them, and re-layouts: 3.76 us -> 3.04 us
  Pallas kernels: 24.4 us -> 24.7 us
    unnamed x6 -> x2, local copies, waits for them, and re-layouts: 3.76 us -> 3.04 us
    pallas_call x1, Pallas kernels: 24.4 us -> 24.7 us  [fused(): pl.pallas_call(functools.partial(kernel, points), out_shape=(jax.ShapeDty...]
where the time goes in v3:
time: 28.6 us; the launch traced here: 28.4 us
  Pallas kernels  24.7 us (86%)
  local copies, waits for them, and re-layouts  3.04 us (11%)
  between operations  0.64 us (2%)
    pallas_call x1, Pallas kernels, fused(): pl.pallas_call(functools.partial(kernel, points), out_shape=(jax.ShapeDty...  24.7 us
    unnamed x2, local copies, waits for them, and re-layouts  3.04 us

profile of v3, /device:TPU:0, one launch (start us, length us, event | category | flops | bytes accessed | tf_op | source)
XLA Modules:
  0.0 28.4 jit_solution(9845893745640866428)
XLA Ops:
  0.6 24.7 %welch_qr.1 = (f32[8,16,16]{2,1,0:T(8,128)}, f32[8,16,256]{2,1,0:T(8,128)}) custom-call(f32[64,8192]{1,0:T(8,128)} %x_hbm.1), custom_call_target="tpu_custom_call" | custom-call | tf_op jit(solution)/shard_map/welch_qr/pallas_call | solution.py:244
  25.4 1.5 %copy.5 = f32[8,16,16]{2,1,0:T(8,128)} copy(f32[8,16,16]{2,1,0:T(8,128)} %get-tuple-element.4) | data formatting | bytes 16384
  26.8 1.6 %copy.6 = f32[8,16,256]{2,1,0:T(8,128)} copy(f32[8,16,256]{2,1,0:T(8,128)} %get-tuple-element.5) | data formatting | bytes 262144

commit v4 on v3

--- a/solution.py
+++ b/solution.py
@@ -58,10 +58,10 @@
 
 
 def kernel(
-    points, x_hbm, factors_ref, modes_ref,
+    points, x_hbm, columns_hbm, gram_ref,
     x_buf, table, part, core_in, y_out, y_in, block_out, blocks,
-    gram_out, gram_in, plane_out, plane_in, upper,
-    in_sem, core_send, core_recv, y_send, y_recv,
+    columns_buf, gram_out, gram_in, plane_out, plane_in,
+    in_sem, columns_sem, core_send, core_recv, y_send, y_recv,
     block_send, block_recv, gram_send, gram_recv, plane_send, plane_recv,
 ):
     aa, ba = lax.axis_index("aa"), lax.axis_index("ba")
@@ -161,6 +161,9 @@
         ],
         axis=1,
     )
+    columns_buf[...] = columns
+    columns_copy = pltpu.make_async_copy(columns_buf, columns_hbm, columns_sem)
+    columns_copy.start()
     high, middle, low = split3(columns)
     contract_last = (((1,), (1,)), ((), ()))
     product = lax.dot_general(
@@ -191,8 +194,16 @@
     ]
     for copy in copies:
         copy.wait_recv()
-    gram = (plane_out[...] + plane_in[2]) + (plane_in[1] + plane_in[3])
-
+    gram_ref[...] = (plane_out[...] + plane_in[2]) + (plane_in[1] + plane_in[3])
+    columns_copy.wait()
+    for copy in sends:
+        copy.wait_send()
+
+
+def finish_kernel(points, gram_ref, columns_hbm, factors_hbm, modes_hbm, columns, upper, factors, modes, sems):
+    load = pltpu.make_async_copy(columns_hbm, columns, sems.at[0])
+    load.start()
+    gram = gram_ref[...]
     lane = lax.broadcasted_iota(jnp.int32, (16, 128), 1) % 16
     row = lax.broadcasted_iota(jnp.int32, (16, 128), 0)
     natural = (row % 8) * 2 + row // 8
@@ -221,34 +232,42 @@
     upper[...] = jnp.zeros_like(upper)
     upper[pl.ds(0, 8, stride=2), :] = upper_all[0:8]
     upper[pl.ds(1, 8, stride=2), :] = upper_all[8:16]
-    factors_ref[...] = jnp.transpose(upper[...])[:, 0:16].reshape(8, 16, 16)
+    factors[...] = jnp.transpose(upper[...])[:, 0:16].reshape(8, 16, 16)
+    factors_copy = pltpu.make_async_copy(factors, factors_hbm, sems.at[1])
+    factors_copy.start()
 
     inverse_all = inverse_all * math.sqrt(points)
-    wide = jnp.where(same, jnp.concatenate([inverse_all] * 8, axis=0), 0.0)
+    row_freq = lax.broadcasted_iota(jnp.int32, (128, 128), 0) // 16
+    lane_freq = lax.broadcasted_iota(jnp.int32, (128, 128), 1) // 16
+    wide = jnp.where(row_freq == lane_freq, jnp.concatenate([inverse_all] * 8, axis=0), 0.0)
     w_high, w_middle, w_low = split3(jnp.transpose(wide))
-    modes = lax.dot_general(
+    load.wait()
+    high, middle, low = split3(columns[...])
+    product = lax.dot_general(
         jnp.concatenate([w_high, w_high, w_middle, w_middle, w_high, w_low], axis=1),
         jnp.concatenate([high, middle, high, middle, low, high], axis=0),
         (((1,), (0,)), ((), ())),
         preferred_element_type=F32,
     )
-    modes_ref[...] = modes.reshape(8, 16, 256)
-    for copy in sends:
-        copy.wait_send()
+    modes[...] = product.reshape(8, 16, 256)
+    modes_copy = pltpu.make_async_copy(modes, modes_hbm, sems.at[2])
+    modes_copy.start()
+    factors_copy.wait()
+    modes_copy.wait()
 
 
 def fused(snapshots):
     points = snapshots.shape[1]
     dma = pltpu.SemaphoreType.DMA
     vmem = pltpu.VMEM
-    return pl.pallas_call(
+    columns, gram = pl.pallas_call(
         functools.partial(kernel, points),
         out_shape=(
-            jax.ShapeDtypeStruct((8, 16, 16), F32),
-            jax.ShapeDtypeStruct((8, 16, 256), F32),
+            jax.ShapeDtypeStruct((128, 256), F32),
+            jax.ShapeDtypeStruct((16, 128), F32),
         ),
         in_specs=[pl.BlockSpec(memory_space=pltpu.HBM)],
-        out_specs=(pl.BlockSpec(memory_space=pltpu.VMEM),) * 2,
+        out_specs=(pl.BlockSpec(memory_space=pl.ANY), pl.BlockSpec(memory_space=pltpu.VMEM)),
         scratch_shapes=[
             vmem((16, 64, 512), F32),
             vmem((48, 192), BF16),
@@ -258,12 +277,13 @@
             vmem((8, 16, 256), F32),
             vmem((8, 2, 16, 128), F32),
             vmem((2, 128, 128), F32),
+            vmem((128, 256), F32),
             vmem((16, 128), F32),
             vmem((8, 16, 128), F32),
             vmem((16, 128), F32),
             vmem((4, 16, 128), F32),
-            vmem((128, 128), F32),
             dma((16,)),
+            dma,
             dma((16,)),
             dma((16,)),
             dma((8,)),
@@ -276,10 +296,28 @@
             dma((4,)),
         ],
         compiler_params=pltpu.CompilerParams(
-            collective_id=0, has_side_effects=True, vmem_limit_bytes=63 * 1024 * 1024
+            collective_id=0, has_side_effects=True, vmem_limit_bytes=53 * 1024 * 1024
         ),
-        name="welch_qr",
+        name="welch_gram",
     )(snapshots)
+    return pl.pallas_call(
+        functools.partial(finish_kernel, points),
+        out_shape=(
+            jax.ShapeDtypeStruct((8, 16, 16), F32),
+            jax.ShapeDtypeStruct((8, 16, 256), F32),
+        ),
+        in_specs=[pl.BlockSpec(memory_space=pltpu.VMEM), pl.BlockSpec(memory_space=pl.ANY)],
+        out_specs=(pl.BlockSpec(memory_space=pl.ANY),) * 2,
+        scratch_shapes=[
+            vmem((128, 256), F32),
+            vmem((128, 128), F32),
+            vmem((8, 16, 16), F32),
+            vmem((8, 16, 256), F32),
+            dma((3,)),
+        ],
+        compiler_params=pltpu.CompilerParams(vmem_limit_bytes=16 * 1024 * 1024),
+        name="factor_modes",
+    )(gram, columns)
 
 
 def local(snapshots):

time: 28.6 us -> 26 us (0.909)
  local copies, waits for them, and re-layouts: 3.04 us -> 0 us
  Pallas kernels: 24.7 us -> 25.2 us
    unnamed x2 -> x0, local copies, waits for them, and re-layouts: 3.04 us -> none
    pallas_call x0 -> x1, Pallas kernels: none -> 1.56 us  [fused(): pl.pallas_call(functools.partial(finish_kernel, points), out_shape=(jax.S...]
    pallas_call x1, Pallas kernels: 24.7 us -> 23.6 us  [fused(): pl.pallas_call(functools.partial(kernel, points), out_shape=(jax.ShapeDty...]
where the time goes in v4:
time: 26 us; the launch traced here: 25.8 us
  Pallas kernels  25.2 us (97%)
  between operations  0.64 us (2%)
    pallas_call x1, Pallas kernels, fused(): pl.pallas_call(functools.partial(kernel, points), out_shape=(jax.ShapeDty...  23.6 us
    pallas_call x1, Pallas kernels, fused(): pl.pallas_call(functools.partial(finish_kernel, points), out_shape=(jax.S...  1.56 us

profile of v4, /device:TPU:0, one launch (start us, length us, event | category | flops | bytes accessed | tf_op | source)
XLA Modules:
  0.0 25.8 jit_solution(11557111026872948913)
XLA Ops:
  0.6 23.6 %welch_gram.1 = (f32[128,256]{1,0:T(8,128)S(1)}, f32[16,128]{1,0:T(8,128)S(1)}) custom-call(f32[64,8192]{1,0:T(8,128)} %x_hbm.1), custom_call_target="tpu_custom_call" | custom-call | tf_op jit(solution)/shard_map/welch_gram/pallas_call | solution.py:263
  24.2 1.6 %factor_modes.1 = (f32[8,16,16]{2,1,0:T(8,128)}, f32[8,16,256]{2,1,0:T(8,128)}) custom-call(f32[16,128]{1,0:T(8,128)S(1)} %get-tuple-element.4.gram_ref, f32[128,256]{1,0:T(8,128)S(1)} %get-tuple-element.5.columns_hbm), custom_call_target="tpu_custom_call" | custom-call | tf_op jit(solution)/shard_map/factor_modes/pallas_call | solution.py:303

commit v5 on v4

--- a/solution.py
+++ b/solution.py
@@ -15,11 +15,11 @@
 
 STEPS = ((2, 0), (2, 1), (1, 0), (1, 1), (3, 0), (3, 1), (0, 1), (0, 0))
 GROUPS = (
-    ((0, 1), ()),
-    ((2, 3), ()),
-    ((4, 5, 6, 7), (0, 1, 2, 3)),
-    ((8, 9, 10, 11), (4, 5, 6, 7)),
-    ((12, 13, 14, 15), ()),
+    ((0,), ()),
+    ((1,), ()),
+    ((2, 3), (0,)),
+    ((4, 5), (1, 2)),
+    ((6, 7), (3, 4, 5, 6, 7)),
 )
 
 
@@ -77,20 +77,17 @@
     ]
     line_ids = [(((z + dz) % 4) * 2 + x, ba) for dz in range(4)]
 
-    loads = []
-    for tile in range(16):
-        row, k = tile // 8, tile % 8
-        side = (1 - y) if row == 0 else y
-        start = pl.multiple_of(owners[k] * 1024 + side * 512, 512)
-        load = pltpu.make_async_copy(x_hbm.at[:, pl.ds(start, 512)], x_buf.at[tile], in_sem.at[tile])
-        load.start()
-        loads.append(load)
-
     barrier = pltpu.get_barrier_semaphore()
     peers = [(owner, ba) for owner in owners[:-1]]
     peers += [plane_ids[i] for i in range(1, 8) if plane[i] != (1, 0, 0)]
     for peer in peers:
         pl.semaphore_signal(barrier, inc=1, device_id=peer, device_id_type=MESH)
+    loads = []
+    for k in range(8):
+        start = pl.multiple_of(owners[k] * 1024, 1024)
+        load = pltpu.make_async_copy(x_hbm.at[:, pl.ds(start, 1024)], x_buf.at[k], in_sem.at[k])
+        load.start()
+        loads.append(load)
     table[...] = split_table(ba, points)
 
     sends = []
@@ -109,7 +106,7 @@
 
     def send_y(k):
         core_copies[k].wait_recv()
-        y_out[k] = part[k, core] + core_in[k]
+        y_out[k] = part[k, core, 1 - y] + core_in[k, 1 - y]
         y_copies.append(remote(y_out.at[k], y_in.at[k], y_send.at[k], y_recv.at[k], y_peer))
 
     for group, ready in GROUPS:
@@ -119,8 +116,9 @@
         rows = jnp.dot(table[...], jnp.concatenate(terms, axis=1), preferred_element_type=F32)
         total = rows[0:16] + rows[16:32] + rows[32:48]
         for n, tile in enumerate(group):
-            part[tile, 0] = total[:, n * 512:n * 512 + 256]
-            part[tile, 1] = total[:, n * 512 + 256:n * 512 + 512]
+            for half in range(4):
+                at = n * 1024 + half * 256
+                part[tile, half % 2, half // 2] = total[:, at:at + 256]
         if group[0] == 0:
             pl.semaphore_wait(barrier, len(peers))
         for tile in group:
@@ -135,9 +133,8 @@
 
     block_copies = []
     for k in range(8):
-        core_copies[8 + k].wait_recv()
         y_copies[k].wait_recv()
-        total = part[8 + k, core] + core_in[8 + k] + y_in[k]
+        total = part[k, core, y] + core_in[k, y] + y_in[k]
         mine = pl.ds(pl.multiple_of(aa * 16, 16), 16)
         if k == 7:
             blocks[0, mine, :] = total[:, 0:128]
@@ -185,6 +182,8 @@
     copies = [
         remote(gram_out, gram_in.at[i], gram_send.at[i], gram_recv.at[i], plane_ids[i]) for i in range(1, 8)
     ]
+    for copy in sends[:-7]:
+        copy.wait_send()
     for copy in copies:
         copy.wait_recv()
     pairs = [gram_out[...] + gram_in[1]] + [gram_in[i] + gram_in[i + 1] for i in (2, 4, 6)]
@@ -192,11 +191,13 @@
     copies = [
         remote(plane_out, plane_in.at[i], plane_send.at[i], plane_recv.at[i], line_ids[i]) for i in range(1, 4)
     ]
+    columns_copy.wait()
+    for copy in sends[-10:-3]:
+        copy.wait_send()
     for copy in copies:
         copy.wait_recv()
     gram_ref[...] = (plane_out[...] + plane_in[2]) + (plane_in[1] + plane_in[3])
-    columns_copy.wait()
-    for copy in sends:
+    for copy in sends[-3:]:
         copy.wait_send()
 
 
@@ -269,10 +270,10 @@
         in_specs=[pl.BlockSpec(memory_space=pltpu.HBM)],
         out_specs=(pl.BlockSpec(memory_space=pl.ANY), pl.BlockSpec(memory_space=pltpu.VMEM)),
         scratch_shapes=[
-            vmem((16, 64, 512), F32),
+            vmem((8, 64, 1024), F32),
             vmem((48, 192), BF16),
-            vmem((16, 2, 16, 256), F32),
-            vmem((16, 16, 256), F32),
+            vmem((8, 2, 2, 16, 256), F32),
+            vmem((8, 2, 16, 256), F32),
             vmem((8, 16, 256), F32),
             vmem((8, 16, 256), F32),
             vmem((8, 2, 16, 128), F32),
@@ -282,10 +283,10 @@
             vmem((8, 16, 128), F32),
             vmem((16, 128), F32),
             vmem((4, 16, 128), F32),
-            dma((16,)),
+            dma((8,)),
             dma,
-            dma((16,)),
-            dma((16,)),
+            dma((8,)),
+            dma((8,)),
             dma((8,)),
             dma((8,)),
             dma((8,)),

time: 26 us -> 26 us (level)
  no operation moved by 1% of the time
where the time goes in v5:
time: 26 us; the launch traced here: 25.9 us
  Pallas kernels  25.2 us (97%)
  between operations  0.64 us (2%)
    pallas_call x1, Pallas kernels, fused(): pl.pallas_call(functools.partial(kernel, points), out_shape=(jax.ShapeDty...  23.7 us
    pallas_call x1, Pallas kernels, fused(): pl.pallas_call(functools.partial(finish_kernel, points), out_shape=(jax.S...  1.56 us

profile of v5, /device:TPU:0, one launch (start us, length us, event | category | flops | bytes accessed | tf_op | source)
XLA Modules:
  0.0 25.9 jit_solution(12498273999646840688)
XLA Ops:
  0.6 23.7 %welch_gram.1 = (f32[128,256]{1,0:T(8,128)S(1)}, f32[16,128]{1,0:T(8,128)S(1)}) custom-call(f32[64,8192]{1,0:T(8,128)} %x_hbm.1), custom_call_target="tpu_custom_call" | custom-call | tf_op jit(solution)/shard_map/welch_gram/pallas_call | solution.py:264
  24.3 1.6 %factor_modes.1 = (f32[8,16,16]{2,1,0:T(8,128)}, f32[8,16,256]{2,1,0:T(8,128)}) custom-call(f32[16,128]{1,0:T(8,128)S(1)} %get-tuple-element.4.gram_ref, f32[128,256]{1,0:T(8,128)S(1)} %get-tuple-element.5.columns_hbm), custom_call_target="tpu_custom_call" | custom-call | tf_op jit(solution)/shard_map/factor_modes/pallas_call | solution.py:304

commit v6 on v5

--- a/solution.py
+++ b/solution.py
@@ -14,12 +14,10 @@
 F32 = jnp.float32
 
 STEPS = ((2, 0), (2, 1), (1, 0), (1, 1), (3, 0), (3, 1), (0, 1), (0, 0))
-GROUPS = (
-    ((0,), ()),
-    ((1,), ()),
-    ((2, 3), (0,)),
-    ((4, 5), (1, 2)),
-    ((6, 7), (3, 4, 5, 6, 7)),
+GROUPS = ((0,), (1, 2), (3, 4), (5, 6, 7))
+DIRECT = 3
+STAGES = (("y", 3), ("y", 4), ("b", 0), ("y", 5), ("b", 1), ("y", 6), ("b", 2), ("y", 7)) + tuple(
+    ("b", k) for k in range(3, 8)
 )
 
 
@@ -59,9 +57,9 @@
 
 def kernel(
     points, x_hbm, columns_hbm, gram_ref,
-    x_buf, table, part, core_in, y_out, y_in, block_out, blocks,
+    x_buf, table, part, core_in, y_out, y_in, cross_in, block_out, blocks,
     columns_buf, gram_out, gram_in, plane_out, plane_in,
-    in_sem, columns_sem, core_send, core_recv, y_send, y_recv,
+    in_sem, columns_sem, cross_send, cross_recv, core_send, core_recv, y_send, y_recv,
     block_send, block_recv, gram_send, gram_recv, plane_send, plane_recv,
 ):
     aa, ba = lax.axis_index("aa"), lax.axis_index("ba")
@@ -70,6 +68,7 @@
     other_core = 1 - core
     core_peer = (aa, y * 2 + other_core)
     y_peer = (aa, (1 - y) * 2 + core)
+    cross_peer = (aa, (1 - y) * 2 + other_core)
     owners = [((z + dz) % 4) * 2 + (x + dx) % 2 for dz, dx in STEPS]
     plane = [(i // 4, i // 2 % 2, i % 2) for i in range(8)]
     plane_ids = [
@@ -101,15 +100,14 @@
         sends.append(copy)
         return copy
 
-    core_copies = []
-    y_copies = []
+    core_copies, y_copies, cross_copies = {}, {}, {}
 
     def send_y(k):
         core_copies[k].wait_recv()
         y_out[k] = part[k, core, 1 - y] + core_in[k, 1 - y]
-        y_copies.append(remote(y_out.at[k], y_in.at[k], y_send.at[k], y_recv.at[k], y_peer))
-
-    for group, ready in GROUPS:
+        y_copies[k] = remote(y_out.at[k], y_in.at[k], y_send.at[k], y_recv.at[k], y_peer)
+
+    for group in GROUPS:
         for tile in group:
             loads[tile].wait()
         terms = [jnp.concatenate(split3(x_buf[tile]), axis=0) for tile in group]
@@ -122,20 +120,37 @@
         if group[0] == 0:
             pl.semaphore_wait(barrier, len(peers))
         for tile in group:
-            core_copies.append(
-                remote(
+            if tile < DIRECT:
+                y_copies[tile] = remote(
+                    part.at[tile, core, 1 - y], y_in.at[tile], y_send.at[tile], y_recv.at[tile], y_peer
+                )
+                cross_copies[tile] = remote(
+                    part.at[tile, other_core, 1 - y], cross_in.at[tile],
+                    cross_send.at[tile], cross_recv.at[tile], cross_peer,
+                )
+                core_copies[tile] = remote(
+                    part.at[tile, other_core, y], core_in.at[tile, y],
+                    core_send.at[tile], core_recv.at[tile], core_peer,
+                )
+            else:
+                core_copies[tile] = remote(
                     part.at[tile, other_core], core_in.at[tile],
                     core_send.at[tile], core_recv.at[tile], core_peer,
                 )
-            )
-        for k in ready:
+
+    block_copies = []
+    mine = pl.ds(pl.multiple_of(aa * 16, 16), 16)
+    for stage, k in STAGES:
+        if stage == "y":
             send_y(k)
-
-    block_copies = []
-    for k in range(8):
+            continue
         y_copies[k].wait_recv()
-        total = part[k, core, y] + core_in[k, y] + y_in[k]
-        mine = pl.ds(pl.multiple_of(aa * 16, 16), 16)
+        total = part[k, core, y]
+        if k < DIRECT:
+            core_copies[k].wait_recv()
+            cross_copies[k].wait_recv()
+            total = total + cross_in[k]
+        total = total + core_in[k, y] + y_in[k]
         if k == 7:
             blocks[0, mine, :] = total[:, 0:128]
             blocks[1, mine, :] = total[:, 128:256]
@@ -276,6 +291,7 @@
             vmem((8, 2, 16, 256), F32),
             vmem((8, 16, 256), F32),
             vmem((8, 16, 256), F32),
+            vmem((DIRECT, 16, 256), F32),
             vmem((8, 2, 16, 128), F32),
             vmem((2, 128, 128), F32),
             vmem((128, 256), F32),
@@ -285,6 +301,8 @@
             vmem((4, 16, 128), F32),
             dma((8,)),
             dma,
+            dma((DIRECT,)),
+            dma((DIRECT,)),
             dma((8,)),
             dma((8,)),
             dma((8,)),

time: 26 us -> 26.7 us (1.027)
  Pallas kernels: 25.2 us -> 25.9 us
    pallas_call x1, Pallas kernels: 23.7 us -> 24.3 us  [fused(): pl.pallas_call(functools.partial(kernel, points), out_shape=(jax.ShapeDty...]
where the time goes in v6:
time: 26.7 us; the launch traced here: 26.5 us
  Pallas kernels  25.9 us (97%)
  between operations  0.64 us (2%)
    pallas_call x1, Pallas kernels, fused(): pl.pallas_call(functools.partial(kernel, points), out_shape=(jax.ShapeDty...  24.3 us
    pallas_call x1, Pallas kernels, fused(): pl.pallas_call(functools.partial(finish_kernel, points), out_shape=(jax.S...  1.56 us

profile of v6, /device:TPU:0, one launch (start us, length us, event | category | flops | bytes accessed | tf_op | source)
XLA Modules:
  0.0 26.5 jit_solution(9014612788882010400)
XLA Ops:
  0.6 24.3 %welch_gram.1 = (f32[128,256]{1,0:T(8,128)S(1)}, f32[16,128]{1,0:T(8,128)S(1)}) custom-call(f32[64,8192]{1,0:T(8,128)} %x_hbm.1), custom_call_target="tpu_custom_call" | custom-call | tf_op jit(solution)/shard_map/welch_gram/pallas_call | solution.py:279
  24.9 1.6 %factor_modes.1 = (f32[8,16,16]{2,1,0:T(8,128)}, f32[8,16,256]{2,1,0:T(8,128)}) custom-call(f32[16,128]{1,0:T(8,128)S(1)} %get-tuple-element.4.gram_ref, f32[128,256]{1,0:T(8,128)S(1)} %get-tuple-element.5.columns_hbm), custom_call_target="tpu_custom_call" | custom-call | tf_op jit(solution)/shard_map/factor_modes/pallas_call | solution.py:322

commit v7 on v6

--- a/solution.py
+++ b/solution.py
@@ -14,10 +14,11 @@
 F32 = jnp.float32
 
 STEPS = ((2, 0), (2, 1), (1, 0), (1, 1), (3, 0), (3, 1), (0, 1), (0, 0))
-GROUPS = ((0,), (1, 2), (3, 4), (5, 6, 7))
-DIRECT = 3
-STAGES = (("y", 3), ("y", 4), ("b", 0), ("y", 5), ("b", 1), ("y", 6), ("b", 2), ("y", 7)) + tuple(
-    ("b", k) for k in range(3, 8)
+DIRECT = 1
+STAGES = (
+    ("c", 0), ("c", 1), ("c", 2), ("c", 3), ("y", 1), ("c", 4), ("y", 2), ("b", 0), ("c", 5), ("y", 3),
+    ("c", 6), ("y", 4), ("b", 1), ("c", 7), ("y", 5), ("b", 2), ("y", 6), ("b", 3), ("y", 7), ("b", 4),
+    ("b", 5), ("b", 6), ("b", 7),
 )
 
 
@@ -107,40 +108,39 @@
         y_out[k] = part[k, core, 1 - y] + core_in[k, 1 - y]
         y_copies[k] = remote(y_out.at[k], y_in.at[k], y_send.at[k], y_recv.at[k], y_peer)
 
-    for group in GROUPS:
-        for tile in group:
-            loads[tile].wait()
-        terms = [jnp.concatenate(split3(x_buf[tile]), axis=0) for tile in group]
-        rows = jnp.dot(table[...], jnp.concatenate(terms, axis=1), preferred_element_type=F32)
+    def compute(tile):
+        loads[tile].wait()
+        terms = jnp.concatenate(split3(x_buf[tile]), axis=0)
+        rows = jnp.dot(table[...], terms, preferred_element_type=F32)
         total = rows[0:16] + rows[16:32] + rows[32:48]
-        for n, tile in enumerate(group):
-            for half in range(4):
-                at = n * 1024 + half * 256
-                part[tile, half % 2, half // 2] = total[:, at:at + 256]
-        if group[0] == 0:
+        for half in range(4):
+            part[tile, half % 2, half // 2] = total[:, half * 256:half * 256 + 256]
+        if tile == 0:
             pl.semaphore_wait(barrier, len(peers))
-        for tile in group:
-            if tile < DIRECT:
-                y_copies[tile] = remote(
-                    part.at[tile, core, 1 - y], y_in.at[tile], y_send.at[tile], y_recv.at[tile], y_peer
-                )
-                cross_copies[tile] = remote(
-                    part.at[tile, other_core, 1 - y], cross_in.at[tile],
-                    cross_send.at[tile], cross_recv.at[tile], cross_peer,
-                )
-                core_copies[tile] = remote(
-                    part.at[tile, other_core, y], core_in.at[tile, y],
-                    core_send.at[tile], core_recv.at[tile], core_peer,
-                )
-            else:
-                core_copies[tile] = remote(
-                    part.at[tile, other_core], core_in.at[tile],
-                    core_send.at[tile], core_recv.at[tile], core_peer,
-                )
+        if tile < DIRECT:
+            y_copies[tile] = remote(
+                part.at[tile, core, 1 - y], y_in.at[tile], y_send.at[tile], y_recv.at[tile], y_peer
+            )
+            cross_copies[tile] = remote(
+                part.at[tile, other_core, 1 - y], cross_in.at[tile],
+                cross_send.at[tile], cross_recv.at[tile], cross_peer,
+            )
+            core_copies[tile] = remote(
+                part.at[tile, other_core, y], core_in.at[tile, y],
+                core_send.at[tile], core_recv.at[tile], core_peer,
+            )
+        else:
+            core_copies[tile] = remote(
+                part.at[tile, other_core], core_in.at[tile],
+                core_send.at[tile], core_recv.at[tile], core_peer,
+            )
 
     block_copies = []
     mine = pl.ds(pl.multiple_of(aa * 16, 16), 16)
     for stage, k in STAGES:
+        if stage == "c":
+            compute(k)
+            continue
         if stage == "y":
             send_y(k)
             continue

time: 26.7 us -> 27.6 us (1.034)
  Pallas kernels: 25.9 us -> 26.9 us
    pallas_call x1, Pallas kernels: 24.3 us -> 25.3 us  [fused(): pl.pallas_call(functools.partial(kernel, points), out_shape=(jax.ShapeDty...]
where the time goes in v7:
time: 27.6 us; the launch traced here: 27.5 us
  Pallas kernels  26.9 us (97%)
  between operations  0.64 us (2%)
    pallas_call x1, Pallas kernels, fused(): pl.pallas_call(functools.partial(kernel, points), out_shape=(jax.ShapeDty...  25.3 us
    pallas_call x1, Pallas kernels, fused(): pl.pallas_call(functools.partial(finish_kernel, points), out_shape=(jax.S...  1.56 us

profile of v7, /device:TPU:0, one launch (start us, length us, event | category | flops | bytes accessed | tf_op | source)
XLA Modules:
  0.0 27.5 jit_solution(18149479065433896860)
XLA Ops:
  0.6 25.3 %welch_gram.1 = (f32[128,256]{1,0:T(8,128)S(1)}, f32[16,128]{1,0:T(8,128)S(1)}) custom-call(f32[64,8192]{1,0:T(8,128)} %x_hbm.1), custom_call_target="tpu_custom_call" | custom-call | tf_op jit(solution)/shard_map/welch_gram/pallas_call | solution.py:279
  25.9 1.6 %factor_modes.1 = (f32[8,16,16]{2,1,0:T(8,128)}, f32[8,16,256]{2,1,0:T(8,128)}) custom-call(f32[16,128]{1,0:T(8,128)S(1)} %get-tuple-element.4.gram_ref, f32[128,256]{1,0:T(8,128)S(1)} %get-tuple-element.5.columns_hbm), custom_call_target="tpu_custom_call" | custom-call | tf_op jit(solution)/shard_map/factor_modes/pallas_call | solution.py:322

commit v8 on v5

--- a/solution.py
+++ b/solution.py
@@ -15,11 +15,8 @@
 
 STEPS = ((2, 0), (2, 1), (1, 0), (1, 1), (3, 0), (3, 1), (0, 1), (0, 0))
 GROUPS = (
-    ((0,), ()),
-    ((1,), ()),
-    ((2, 3), (0,)),
-    ((4, 5), (1, 2)),
-    ((6, 7), (3, 4, 5, 6, 7)),
+    ((0, 1, 2, 3), ()),
+    ((4, 5, 6, 7), (0, 1, 2, 3, 4, 5, 6, 7)),
 )
 
 
@@ -109,6 +106,7 @@
         y_out[k] = part[k, core, 1 - y] + core_in[k, 1 - y]
         y_copies.append(remote(y_out.at[k], y_in.at[k], y_send.at[k], y_recv.at[k], y_peer))
 
+    pl.semaphore_wait(barrier, len(peers))
     for group, ready in GROUPS:
         for tile in group:
             loads[tile].wait()
@@ -119,8 +117,6 @@
             for half in range(4):
                 at = n * 1024 + half * 256
                 part[tile, half % 2, half // 2] = total[:, at:at + 256]
-        if group[0] == 0:
-            pl.semaphore_wait(barrier, len(peers))
         for tile in group:
             core_copies.append(
                 remote(

time: 26 us -> 25.8 us (level)
  no operation moved by 1% of the time
where the time goes in v8:
time: 25.8 us; the launch traced here: 25.7 us
  Pallas kernels  25 us (97%)
  between operations  0.64 us (2%)
    pallas_call x1, Pallas kernels, fused(): pl.pallas_call(functools.partial(kernel, points), out_shape=(jax.ShapeDty...  23.5 us
    pallas_call x1, Pallas kernels, fused(): pl.pallas_call(functools.partial(finish_kernel, points), out_shape=(jax.S...  1.56 us

profile of v8, /device:TPU:0, one launch (start us, length us, event | category | flops | bytes accessed | tf_op | source)
XLA Modules:
  0.0 25.7 jit_solution(2199007483080934013)
XLA Ops:
  0.6 23.5 %welch_gram.1 = (f32[128,256]{1,0:T(8,128)S(1)}, f32[16,128]{1,0:T(8,128)S(1)}) custom-call(f32[64,8192]{1,0:T(8,128)} %x_hbm.1), custom_call_target="tpu_custom_call" | custom-call | tf_op jit(solution)/shard_map/welch_gram/pallas_call | solution.py:260
  24.1 1.6 %factor_modes.1 = (f32[8,16,16]{2,1,0:T(8,128)}, f32[8,16,256]{2,1,0:T(8,128)}) custom-call(f32[16,128]{1,0:T(8,128)S(1)} %get-tuple-element.4.gram_ref, f32[128,256]{1,0:T(8,128)S(1)} %get-tuple-element.5.columns_hbm), custom_call_target="tpu_custom_call" | custom-call | tf_op jit(solution)/shard_map/factor_modes/pallas_call | solution.py:300

commit v9 on v8

--- a/solution.py
+++ b/solution.py
@@ -14,10 +14,8 @@
 F32 = jnp.float32
 
 STEPS = ((2, 0), (2, 1), (1, 0), (1, 1), (3, 0), (3, 1), (0, 1), (0, 0))
-GROUPS = (
-    ((0, 1, 2, 3), ()),
-    ((4, 5, 6, 7), (0, 1, 2, 3, 4, 5, 6, 7)),
-)
+GROUPS = ((0, 1, 2, 3), (4, 5, 6, 7))
+STRAIGHT = (4, 5, 6)
 
 
 def spectral_table(block_len, points):
@@ -68,6 +66,7 @@
     core_peer = (aa, y * 2 + other_core)
     y_peer = (aa, (1 - y) * 2 + core)
     owners = [((z + dz) % 4) * 2 + (x + dx) % 2 for dz, dx in STEPS]
+    sources = [((z + 4 - dz) % 4) * 2 + (x + 2 - dx) % 2 for dz, dx in STEPS]
     plane = [(i // 4, i // 2 % 2, i % 2) for i in range(8)]
     plane_ids = [
         (z * 2 + (x + dx) % 2, ((y + dy) % 2) * 2 + (core + dc) % 2) for dx, dy, dc in plane
@@ -77,6 +76,7 @@
     barrier = pltpu.get_barrier_semaphore()
     peers = [(owner, ba) for owner in owners[:-1]]
     peers += [plane_ids[i] for i in range(1, 8) if plane[i] != (1, 0, 0)]
+    peers += [(sources[k], (1 - y) * 2 + core) for k in STRAIGHT if STEPS[k][0]]
     for peer in peers:
         pl.semaphore_signal(barrier, inc=1, device_id=peer, device_id_type=MESH)
     loads = []
@@ -99,15 +99,15 @@
         return copy
 
     core_copies = []
-    y_copies = []
-
-    def send_y(k):
+    y_copies = {}
+
+    def send_y(k, device):
         core_copies[k].wait_recv()
         y_out[k] = part[k, core, 1 - y] + core_in[k, 1 - y]
-        y_copies.append(remote(y_out.at[k], y_in.at[k], y_send.at[k], y_recv.at[k], y_peer))
+        y_copies[k] = remote(y_out.at[k], y_in.at[k], y_send.at[k], y_recv.at[k], device)
 
     pl.semaphore_wait(barrier, len(peers))
-    for group, ready in GROUPS:
+    for group in GROUPS:
         for tile in group:
             loads[tile].wait()
         terms = [jnp.concatenate(split3(x_buf[tile]), axis=0) for tile in group]
@@ -124,28 +124,39 @@
                     core_send.at[tile], core_recv.at[tile], core_peer,
                 )
             )
-        for k in ready:
-            send_y(k)
-
     block_copies = []
-    for k in range(8):
+    mine = pl.ds(pl.multiple_of(aa * 16, 16), 16)
+
+    def send_block(k, total):
+        block_out[k, 0] = total[:, 0:128]
+        block_out[k, 1] = total[:, 128:256]
+        block_copies.append(
+            remote(
+                block_out.at[k], blocks.at[:, mine, :],
+                block_send.at[k], block_recv.at[k], (owners[k], ba),
+            )
+        )
+
+    for k in (0, 1, 2, 3):
+        send_y(k, y_peer)
+    for k in STRAIGHT:
+        send_y(k, (owners[k], (1 - y) * 2 + core))
+        send_block(k, part[k, core, y] + core_in[k, y])
+    send_y(7, y_peer)
+    for k in (0, 1, 2, 3):
         y_copies[k].wait_recv()
-        total = part[k, core, y] + core_in[k, y] + y_in[k]
-        mine = pl.ds(pl.multiple_of(aa * 16, 16), 16)
-        if k == 7:
-            blocks[0, mine, :] = total[:, 0:128]
-            blocks[1, mine, :] = total[:, 128:256]
-        else:
-            block_out[k, 0] = total[:, 0:128]
-            block_out[k, 1] = total[:, 128:256]
-            block_copies.append(
-                remote(
-                    block_out.at[k], blocks.at[:, mine, :],
-                    block_send.at[k], block_recv.at[k], (owners[k], ba),
-                )
-            )
+        send_block(k, part[k, core, y] + core_in[k, y] + y_in[k])
+    y_copies[7].wait_recv()
+    total = part[7, core, y] + core_in[7, y] + y_in[7]
+    blocks[0, mine, :] = total[:, 0:128]
+    blocks[1, mine, :] = total[:, 128:256]
     for copy in block_copies:
         copy.wait_recv()
+    for k in STRAIGHT:
+        y_copies[k].wait_recv()
+        theirs = pl.ds(pl.multiple_of(sources[k] * 16, 16), 16)
+        blocks[0, theirs, :] += y_in[k, :, 0:128]
+        blocks[1, theirs, :] += y_in[k, :, 128:256]
 
     columns = jnp.concatenate(
         [

time: 25.8 us -> 25.2 us (0.977)
  Pallas kernels: 25 us -> 24.4 us
    pallas_call x1, Pallas kernels: 23.5 us -> 22.9 us  [fused(): pl.pallas_call(functools.partial(kernel, points), out_shape=(jax.ShapeDty...]
where the time goes in v9:
time: 25.2 us; the launch traced here: 25.1 us
  Pallas kernels  24.4 us (97%)
  between operations  0.64 us (3%)
    pallas_call x1, Pallas kernels, fused(): pl.pallas_call(functools.partial(kernel, points), out_shape=(jax.ShapeDty...  22.9 us
    pallas_call x1, Pallas kernels, fused(): pl.pallas_call(functools.partial(finish_kernel, points), out_shape=(jax.S...  1.56 us

profile of v9, /device:TPU:0, one launch (start us, length us, event | category | flops | bytes accessed | tf_op | source)
XLA Modules:
  0.0 25.1 jit_solution(9519035671602911370)
XLA Ops:
  0.6 22.9 %welch_gram.1 = (f32[128,256]{1,0:T(8,128)S(1)}, f32[16,128]{1,0:T(8,128)S(1)}) custom-call(f32[64,8192]{1,0:T(8,128)} %x_hbm.1), custom_call_target="tpu_custom_call" | custom-call | tf_op jit(solution)/shard_map/welch_gram/pallas_call | solution.py:271
  23.5 1.6 %factor_modes.1 = (f32[8,16,16]{2,1,0:T(8,128)}, f32[8,16,256]{2,1,0:T(8,128)}) custom-call(f32[16,128]{1,0:T(8,128)S(1)} %get-tuple-element.4.gram_ref, f32[128,256]{1,0:T(8,128)S(1)} %get-tuple-element.5.columns_hbm), custom_call_target="tpu_custom_call" | custom-call | tf_op jit(solution)/shard_map/factor_modes/pallas_call | solution.py:311

commit v10 on v9

--- a/solution.py
+++ b/solution.py
@@ -15,7 +15,8 @@
 
 STEPS = ((2, 0), (2, 1), (1, 0), (1, 1), (3, 0), (3, 1), (0, 1), (0, 0))
 GROUPS = ((0, 1, 2, 3), (4, 5, 6, 7))
-STRAIGHT = (4, 5, 6)
+STRAIGHT = (2, 3, 4, 5, 6)
+REDUCED = (0, 1)
 
 
 def spectral_table(block_len, points):
@@ -53,10 +54,10 @@
 
 
 def kernel(
-    points, x_hbm, columns_hbm, gram_ref,
+    points, x_hbm, columns_ref, gram_ref,
     x_buf, table, part, core_in, y_out, y_in, block_out, blocks,
-    columns_buf, gram_out, gram_in, plane_out, plane_in,
-    in_sem, columns_sem, core_send, core_recv, y_send, y_recv,
+    gram_out, gram_in, plane_out, plane_in,
+    in_sem, core_send, core_recv, y_send, y_recv,
     block_send, block_recv, gram_send, gram_recv, plane_send, plane_recv,
 ):
     aa, ba = lax.axis_index("aa"), lax.axis_index("ba")
@@ -137,13 +138,13 @@
             )
         )
 
-    for k in (0, 1, 2, 3):
+    for k in REDUCED:
         send_y(k, y_peer)
     for k in STRAIGHT:
         send_y(k, (owners[k], (1 - y) * 2 + core))
         send_block(k, part[k, core, y] + core_in[k, y])
     send_y(7, y_peer)
-    for k in (0, 1, 2, 3):
+    for k in REDUCED:
         y_copies[k].wait_recv()
         send_block(k, part[k, core, y] + core_in[k, y] + y_in[k])
     y_copies[7].wait_recv()
@@ -165,9 +166,7 @@
         ],
         axis=1,
     )
-    columns_buf[...] = columns
-    columns_copy = pltpu.make_async_copy(columns_buf, columns_hbm, columns_sem)
-    columns_copy.start()
+    columns_ref[...] = columns
     high, middle, low = split3(columns)
     contract_last = (((1,), (1,)), ((), ()))
     product = lax.dot_general(
@@ -198,7 +197,6 @@
     copies = [
         remote(plane_out, plane_in.at[i], plane_send.at[i], plane_recv.at[i], line_ids[i]) for i in range(1, 4)
     ]
-    columns_copy.wait()
     for copy in sends[-10:-3]:
         copy.wait_send()
     for copy in copies:
@@ -208,9 +206,8 @@
         copy.wait_send()
 
 
-def finish_kernel(points, gram_ref, columns_hbm, factors_hbm, modes_hbm, columns, upper, factors, modes, sems):
-    load = pltpu.make_async_copy(columns_hbm, columns, sems.at[0])
-    load.start()
+def finish_kernel(points, gram_ref, columns_ref, factors_hbm, modes_hbm, upper, factors, modes, sems):
+    high, middle, low = split3(columns_ref[...])
     gram = gram_ref[...]
     lane = lax.broadcasted_iota(jnp.int32, (16, 128), 1) % 16
     row = lax.broadcasted_iota(jnp.int32, (16, 128), 0)
@@ -241,7 +238,7 @@
     upper[pl.ds(0, 8, stride=2), :] = upper_all[0:8]
     upper[pl.ds(1, 8, stride=2), :] = upper_all[8:16]
     factors[...] = jnp.transpose(upper[...])[:, 0:16].reshape(8, 16, 16)
-    factors_copy = pltpu.make_async_copy(factors, factors_hbm, sems.at[1])
+    factors_copy = pltpu.make_async_copy(factors, factors_hbm, sems.at[0])
     factors_copy.start()
 
     inverse_all = inverse_all * math.sqrt(points)
@@ -249,8 +246,6 @@
     lane_freq = lax.broadcasted_iota(jnp.int32, (128, 128), 1) // 16
     wide = jnp.where(row_freq == lane_freq, jnp.concatenate([inverse_all] * 8, axis=0), 0.0)
     w_high, w_middle, w_low = split3(jnp.transpose(wide))
-    load.wait()
-    high, middle, low = split3(columns[...])
     product = lax.dot_general(
         jnp.concatenate([w_high, w_high, w_middle, w_middle, w_high, w_low], axis=1),
         jnp.concatenate([high, middle, high, middle, low, high], axis=0),
@@ -258,7 +253,7 @@
         preferred_element_type=F32,
     )
     modes[...] = product.reshape(8, 16, 256)
-    modes_copy = pltpu.make_async_copy(modes, modes_hbm, sems.at[2])
+    modes_copy = pltpu.make_async_copy(modes, modes_hbm, sems.at[1])
     modes_copy.start()
     factors_copy.wait()
     modes_copy.wait()
@@ -275,7 +270,7 @@
             jax.ShapeDtypeStruct((16, 128), F32),
         ),
         in_specs=[pl.BlockSpec(memory_space=pltpu.HBM)],
-        out_specs=(pl.BlockSpec(memory_space=pl.ANY), pl.BlockSpec(memory_space=pltpu.VMEM)),
+        out_specs=(pl.BlockSpec(memory_space=pltpu.VMEM),) * 2,
         scratch_shapes=[
             vmem((8, 64, 1024), F32),
             vmem((48, 192), BF16),
@@ -285,13 +280,11 @@
             vmem((8, 16, 256), F32),
             vmem((8, 2, 16, 128), F32),
             vmem((2, 128, 128), F32),
-            vmem((128, 256), F32),
             vmem((16, 128), F32),
             vmem((8, 16, 128), F32),
             vmem((16, 128), F32),
             vmem((4, 16, 128), F32),
             dma((8,)),
-            dma,
             dma((8,)),
             dma((8,)),
             dma((8,)),
@@ -314,14 +307,13 @@
             jax.ShapeDtypeStruct((8, 16, 16), F32),
             jax.ShapeDtypeStruct((8, 16, 256), F32),
         ),
-        in_specs=[pl.BlockSpec(memory_space=pltpu.VMEM), pl.BlockSpec(memory_space=pl.ANY)],
+        in_specs=[pl.BlockSpec(memory_space=pltpu.VMEM)] * 2,
         out_specs=(pl.BlockSpec(memory_space=pl.ANY),) * 2,
         scratch_shapes=[
-            vmem((128, 256), F32),
             vmem((128, 128), F32),
             vmem((8, 16, 16), F32),
             vmem((8, 16, 256), F32),
-            dma((3,)),
+            dma((2,)),
         ],
         compiler_params=pltpu.CompilerParams(vmem_limit_bytes=16 * 1024 * 1024),
         name="factor_modes",

time: 25.2 us -> 25.3 us (level)
    pallas_call x1, Pallas kernels: 22.9 us -> 23.2 us  [fused(): pl.pallas_call(functools.partial(kernel, points), out_shape=(jax.ShapeDty...]
    pallas_call x1, Pallas kernels: 1.56 us -> 1.3 us  [fused(): pl.pallas_call(functools.partial(finish_kernel, points), out_shape=(jax.S...]
where the time goes in v10:
time: 25.3 us; the launch traced here: 25.1 us
  Pallas kernels  24.5 us (97%)
  between operations  0.64 us (3%)
    pallas_call x1, Pallas kernels, fused(): pl.pallas_call(functools.partial(kernel, points), out_shape=(jax.ShapeDty...  23.2 us
    pallas_call x1, Pallas kernels, fused(): pl.pallas_call(functools.partial(finish_kernel, points), out_shape=(jax.S...  1.3 us

profile of v10, /device:TPU:0, one launch (start us, length us, event | category | flops | bytes accessed | tf_op | source)
XLA Modules:
  0.0 25.1 jit_solution(7031461440229249049)
XLA Ops:
  0.6 23.2 %welch_gram.1 = (f32[128,256]{1,0:T(8,128)S(1)}, f32[16,128]{1,0:T(8,128)S(1)}) custom-call(f32[64,8192]{1,0:T(8,128)} %x_hbm.1), custom_call_target="tpu_custom_call" | custom-call | tf_op jit(solution)/shard_map/welch_gram/pallas_call | solution.py:266
  23.8 1.3 %factor_modes.1 = (f32[8,16,16]{2,1,0:T(8,128)}, f32[8,16,256]{2,1,0:T(8,128)}) custom-call(f32[16,128]{1,0:T(8,128)S(1)} %get-tuple-element.4.gram_ref, f32[128,256]{1,0:T(8,128)S(1)} %get-tuple-element.5.columns_ref), custom_call_target="tpu_custom_call" | custom-call | tf_op jit(solution)/shard_map/factor_modes/pallas_call | solution.py:304

commit v11 on v10

--- a/solution.py
+++ b/solution.py
@@ -15,8 +15,8 @@
 
 STEPS = ((2, 0), (2, 1), (1, 0), (1, 1), (3, 0), (3, 1), (0, 1), (0, 0))
 GROUPS = ((0, 1, 2, 3), (4, 5, 6, 7))
-STRAIGHT = (2, 3, 4, 5, 6)
-REDUCED = (0, 1)
+STRAIGHT = (4, 5, 6)
+REDUCED = (0, 1, 2, 3)
 
 
 def spectral_table(block_len, points):

time: 25.3 us -> 24.7 us (0.976)
  Pallas kernels: 24.5 us -> 23.9 us
    pallas_call x1, Pallas kernels: 23.2 us -> 22.6 us  [fused(): pl.pallas_call(functools.partial(kernel, points), out_shape=(jax.ShapeDty...]
where the time goes in v11:
time: 24.7 us; the launch traced here: 24.6 us
  Pallas kernels  23.9 us (97%)
  between operations  0.64 us (3%)
    pallas_call x1, Pallas kernels, fused(): pl.pallas_call(functools.partial(kernel, points), out_shape=(jax.ShapeDty...  22.6 us
    pallas_call x1, Pallas kernels, fused(): pl.pallas_call(functools.partial(finish_kernel, points), out_shape=(jax.S...  1.3 us

profile of v11, /device:TPU:0, one launch (start us, length us, event | category | flops | bytes accessed | tf_op | source)
XLA Modules:
  0.0 24.6 jit_solution(14325629072026310630)
XLA Ops:
  0.6 22.6 %welch_gram.1 = (f32[128,256]{1,0:T(8,128)S(1)}, f32[16,128]{1,0:T(8,128)S(1)}) custom-call(f32[64,8192]{1,0:T(8,128)} %x_hbm.1), custom_call_target="tpu_custom_call" | custom-call | tf_op jit(solution)/shard_map/welch_gram/pallas_call | solution.py:266
  23.3 1.3 %factor_modes.1 = (f32[8,16,16]{2,1,0:T(8,128)}, f32[8,16,256]{2,1,0:T(8,128)}) custom-call(f32[16,128]{1,0:T(8,128)S(1)} %get-tuple-element.4.gram_ref, f32[128,256]{1,0:T(8,128)S(1)} %get-tuple-element.5.columns_ref), custom_call_target="tpu_custom_call" | custom-call | tf_op jit(solution)/shard_map/factor_modes/pallas_call | solution.py:304

commit v12 on v11

--- a/solution.py
+++ b/solution.py
@@ -14,7 +14,7 @@
 F32 = jnp.float32
 
 STEPS = ((2, 0), (2, 1), (1, 0), (1, 1), (3, 0), (3, 1), (0, 1), (0, 0))
-GROUPS = ((0, 1, 2, 3), (4, 5, 6, 7))
+GROUPS = ((0, 1), (2, 3, 4), (5, 6, 7))
 STRAIGHT = (4, 5, 6)
 REDUCED = (0, 1, 2, 3)
 

time: 24.7 us -> 25 us (1.012)
  Pallas kernels: 23.9 us -> 24.2 us
    pallas_call x1, Pallas kernels: 22.6 us -> 22.9 us  [fused(): pl.pallas_call(functools.partial(kernel, points), out_shape=(jax.ShapeDty...]
where the time goes in v12:
time: 25 us; the launch traced here: 24.9 us
  Pallas kernels  24.2 us (97%)
  between operations  0.64 us (3%)
    pallas_call x1, Pallas kernels, fused(): pl.pallas_call(functools.partial(kernel, points), out_shape=(jax.ShapeDty...  22.9 us
    pallas_call x1, Pallas kernels, fused(): pl.pallas_call(functools.partial(finish_kernel, points), out_shape=(jax.S...  1.3 us

profile of v12, /device:TPU:0, one launch (start us, length us, event | category | flops | bytes accessed | tf_op | source)
XLA Modules:
  0.0 24.9 jit_solution(1835674000006996280)
XLA Ops:
  0.6 22.9 %welch_gram.1 = (f32[128,256]{1,0:T(8,128)S(1)}, f32[16,128]{1,0:T(8,128)S(1)}) custom-call(f32[64,8192]{1,0:T(8,128)} %x_hbm.1), custom_call_target="tpu_custom_call" | custom-call | tf_op jit(solution)/shard_map/welch_gram/pallas_call | solution.py:266
  23.6 1.3 %factor_modes.1 = (f32[8,16,16]{2,1,0:T(8,128)}, f32[8,16,256]{2,1,0:T(8,128)}) custom-call(f32[16,128]{1,0:T(8,128)S(1)} %get-tuple-element.4.gram_ref, f32[128,256]{1,0:T(8,128)S(1)} %get-tuple-element.5.columns_ref), custom_call_target="tpu_custom_call" | custom-call | tf_op jit(solution)/shard_map/factor_modes/pallas_call | solution.py:304
